TPU v7x, 32 devices: a whole 2x2x4 slice. The times are simulated.
32 devices in a mesh: groups: 2 (over y), ctx: 4 (over z), tp: 2 (over x), rep: 2 (over core).
Axes of the slice: x: 2, y: 2, z: 4, core: 2. Of those that a mesh axis runs over, the one named last changes fastest.
Arguments:
- queries: bfloat16 [4096, 32, 128], P(('groups', 'ctx'), ('tp', 'rep')), parts along dimension 0, may hold values from -64 to 64
- keys: bfloat16 [4096, 8, 128], P(('groups', 'ctx'), 'tp'), parts along dimension 0, may hold values from -13 to 13
- values: bfloat16 [4096, 8, 128], P(('groups', 'ctx'), 'tp'), parts along dimension 0, may hold values from -6 to 6
- lengths: int32 [8], P('groups'), parts along dimension 0, may hold values from 1 to 1024, 2048 in all
- page_ranks: int32 [32], P(('groups', 'ctx')), parts along dimension 0, may hold values from 0 to 3, as said below
Outputs:
- context: bfloat16 [4096, 32, 128], P(('groups', 'ctx'), ('tp', 'rep')), parts along dimension 0
- decode_cache: bfloat16 [8, 4, 128, 2, 8, 128], P(('groups', 'ctx'), None, None, 'rep', 'tp'), parts along dimension 0
There are 2 independent parts, one for each index of `groups`. A program takes and returns all parts, laid end to end along the dimension named above; each array names one. Nothing has to cross between parts.
Inputs may be any that keep to these rules, and one draw needn't show every extreme that they name: `page_ranks`: pages 4 * s to 4 * s + 3 go to distinct decode ranks, for every s; one decode rank receives a page from every s.
All inputs are finite; a program needn't handle non-finite values.
Results may differ from a plain program's by a relative error of at most 0.0037.
Values may be sent and summed in bfloat16 or wider, within the bound.
A program may use at most 128 MiB of HBM per device.

v0:
```python
import jax
import jax.numpy as jnp
from jax import lax
from jax.sharding import PartitionSpec as P

PAGE = 128


neg_fill = -1e30


def segment_of(positions, ends):
    return jnp.sum((positions[:, None] >= ends[None, :]).astype(jnp.int32), axis=1)


def absorb(carry, pieces, start, halves, ends, kv_index, scale):
    key_piece = jnp.take(pieces[0], kv_index, axis=1)
    value_piece = jnp.take(pieces[1], kv_index, axis=1)
    count = pieces[0].shape[0]
    key_pos = jnp.arange(count, dtype=jnp.int32)
    key_seg = segment_of(key_pos, ends)
    updated = []
    for member, state in zip(halves, carry):
        query_half, query_pos, query_seg = member

        def compute(state, query_half=query_half, query_pos=query_pos, query_seg=query_seg):
            running, denom, accum = state
            allowed = (key_seg[None, :] == query_seg[:, None]) & (
                key_pos[None, :] <= query_pos[:, None]
            )
            score = (
                jnp.einsum(
                    "qhd,khd->qhk", query_half, key_piece, preferred_element_type=jnp.float32
                )
                * scale
            )
            score = jnp.where(allowed[:, None, :], score, neg_fill)
            fresh = jnp.maximum(running, jnp.max(score, axis=2))
            weight = jnp.where(allowed[:, None, :], jnp.exp(score - fresh[:, :, None]), 0.0)
            denom = jnp.sum(weight, axis=2)
            product = jnp.einsum(
                "qhk,khd->qhd",
                weight.astype(jnp.bfloat16),
                value_piece,
                preferred_element_type=jnp.float32,
            )
            accum = product
            return (fresh, denom, accum)

        def unchanged(state):
            return state

        updated.append(lax.cond(start <= query_pos[-1], compute, unchanged, state))
    return tuple(updated)


def body(queries, keys, values, lengths, page_ranks):
    tok_dev, heads_dev, head_dim = queries.shape
    kv_dev = keys.shape[1]
    ctx_size = lax.axis_size("ctx")
    rep_size = lax.axis_size("rep")
    place = lax.axis_index("ctx")
    core = lax.axis_index("rep")
    lane = lax.axis_index("tp")
    group = heads_dev * rep_size // kv_dev
    first_head = (lane * rep_size + core) * heads_dev
    kv_index = (first_head + jnp.arange(heads_dev, dtype=jnp.int32)) // group - lane * kv_dev
    ends = jnp.cumsum(lengths)
    half = tok_dev // 2
    scale = head_dim ** (-0.5)
    second = queries[half:]
    first_pos = place * tok_dev + jnp.arange(half, dtype=jnp.int32)
    second_pos = place * tok_dev + half + jnp.arange(half, dtype=jnp.int32)
    halves = (
        (queries[:half], first_pos, segment_of(first_pos, ends)),
        (second, second_pos, segment_of(second_pos, ends)),
    )
    blank = (
        jnp.full((half, heads_dev), neg_fill, jnp.float32),
        jnp.zeros((half, heads_dev), jnp.float32),
        jnp.zeros((half, heads_dev, head_dim), jnp.float32),
    )
    initial = (blank, blank)
    result = absorb(
        initial,
        (
            lax.all_gather(keys, "ctx", axis=0, tiled=True),
            lax.all_gather(values, "ctx", axis=0, tiled=True),
        ),
        jnp.int32(0),
        halves,
        ends,
        kv_index,
        scale,
    )
    outputs = [(accum / denom[:, :, None]).astype(jnp.bfloat16) for running, denom, accum in result]
    second_out = outputs[1]
    context = jnp.concatenate([outputs[0], second_out], axis=0)
    pages_dev = page_ranks.shape[0]
    payload = jnp.where(core == 0, keys, values).reshape(pages_dev, PAGE * kv_dev * head_dim)
    chooser = (page_ranks[None, :] == jnp.arange(ctx_size, dtype=jnp.int32)[:, None]).astype(
        jnp.bfloat16
    )
    outgoing = jnp.dot(chooser, payload, preferred_element_type=jnp.float32).astype(jnp.bfloat16)
    arrived = lax.all_to_all(outgoing, "ctx", split_axis=0, concat_axis=0, tiled=True)
    decode_cache = arrived.reshape(1, ctx_size, PAGE, 1, kv_dev, head_dim)
    return (context, decode_cache)


def solution(mesh):
    in_specs = (
        P(("groups", "ctx"), ("tp", "rep"), None),
        P(("groups", "ctx"), "tp", None),
        P(("groups", "ctx"), "tp", None),
        P("groups"),
        P(("groups", "ctx")),
    )
    out_specs = (
        P(("groups", "ctx"), ("tp", "rep"), None),
        P(("groups", "ctx"), None, None, "rep", "tp", None),
    )
    return jax.shard_map(body, mesh=mesh, in_specs=in_specs, out_specs=out_specs, check_vma=False)
```

profile of v0, /device:TPU:17, one launch (start us, length us, event | category | flops | bytes accessed | tf_op | source)
XLA Modules:
  0.0 187.8 jit_solution(16680275297165810379)
XLA Ops:
  7.2 1.9 %copy.50 = bf16[512,4,128]{2,0,1:T(8,128)(2,1)} copy(bf16[512,4,128]{2,1,0:T(4,128)(2,1)} %param.13) | data formatting | bytes 1048576 | tf_op args[2]
  9.2 1.9 %copy.49 = bf16[512,4,128]{2,0,1:T(8,128)(2,1)} copy(bf16[512,4,128]{2,1,0:T(4,128)(2,1)} %param.12) | data formatting | bytes 1048576 | tf_op args[1]
  15.4 1.3 reshape.190
  16.7 4.6 %all-to-all-start = ((bf16[4,2,32768]{2,1,0:T(2,128)(2,1)}), bf16[4,2,32768]{2,1,0:T(2,128)(2,1)S(1)}, u32[]{:S(2)}, u32[]{:S(2)}) async-start(bf16[4,2,32768]{2,1,0:T(2,128)(2,1)} %reshape.190), calls=%async_computation | async-start | bytes 1048576 | tf_op jit(solution)/shard_map/all_to_all | solution.py:105
  24.6 20.9 %all-to-all-done = bf16[4,2,32768]{2,1,0:T(2,128)(2,1)S(1)} async-done(((bf16[4,2,32768]{2,1,0:T(2,128)(2,1)}), bf16[4,2,32768]{2,1,0:T(2,128)(2,1)S(1)}, u32[]{:S(2)}, u32[]{:S(2)}) %all-to-all-start) | async-done | bytes 524320 | tf_op jit(solution)/shard_map/all_to_all | solution.py:105
  46.0 3.4 %reduce = bf16[4,65536]{1,0:T(4,128)(2,1)S(1)} reduce(bf16[4,1,65536]{2,1,0:T(2,128)(2,1)S(1)} %reshape.191, bf16[]{:T(256)} %constant.79), dimensions={1}, to_apply=%all_to_all.7.reduce_sub_computation | reduce | bytes 1048578 | tf_op jit(solution)/shard_map/all_to_all | solution.py:105
  49.4 1.3 reshape.164
  50.7 14.5 %all-gather.5.cloned.1.call-done = bf16[2048,4,128]{2,0,1:T(8,128)(2,1)} async-done(((bf16[512,4,128]{2,0,1:T(8,128)(2,1)}), bf16[2048,4,128]{2,0,1:T(8,128)(2,1)}) %all-gather.5.cloned.1.call-update) | async-done | bytes 2097168 | tf_op jit(solution)/shard_map/all_gather | solution.py:88
  65.2 4.6 %gather_fusion.1 = bf16[8,2048,128]{2,1,0:T(8,128)(2,1)} fusion(bf16[2048,4,128]{2,0,1:T(8,128)(2,1)} %all-gather.5.cloned.1.call-done, s32[1024]{0:T(1024)S(1)} %pad_clamp_fusion), kind=kCustom, calls=%fused_computation.1.clone | custom fusion | bytes 8388640 | tf_op jit(solution)/shard_map/jit(_take)/gather | solution.py:18
  69.8 43.4 %all-gather.3.cloned.1.call-done = bf16[2048,4,128]{2,0,1:T(8,128)(2,1)} async-done(((bf16[512,4,128]{2,0,1:T(8,128)(2,1)}), bf16[2048,4,128]{2,0,1:T(8,128)(2,1)}) %all-gather.3.cloned.1.call-update) | async-done | bytes 2097168 | tf_op jit(solution)/shard_map/all_gather | solution.py:87
  113.2 4.6 %gather_fusion = bf16[8,2048,128]{2,1,0:T(8,128)(2,1)} fusion(bf16[2048,4,128]{2,0,1:T(8,128)(2,1)} %all-gather.3.cloned.1.call-done, s32[1024]{0:T(1024)S(1)} %pad_clamp_fusion), kind=kCustom, calls=%fused_computation.clone | custom fusion | bytes 8388640 | tf_op jit(solution)/shard_map/jit(_take)/gather | solution.py:17
  117.8 7.5 %select_bitcast_fusion = (bf16[2048,8,128]{2,0,1:T(8,128)(2,1)}, bf16[2048,8,128]{2,0,1:T(8,128)(2,1)}) fusion(bf16[8,2048,128]{2,1,0:T(8,128)(2,1)} %gather_fusion.1, pred[8]{0:T(512)(128)(4,1)S(1)} %get-tuple-element.141, bf16[8,2048,128]{2,1,0:T(8,128)(2,1)} %gather_fusion), kind=kLoop, calls=%fused_computation.34 | loop fusion | flops 4194304 | bytes 16777224 | tf_op jit(solution)/shard_map/jit(_take)/select_n | solution.py:18
  125.3 26.7 %conditional.3 = (f32[256,8]{0,1:T(8,128)S(1)}, f32[256,8,128]{2,1,0:T(8,128)S(1)}) conditional(s32[]{:T(128)} %bitcast.9, () %tuple.27, (s32[2048]{0:T(1024)S(1)}, s32[256,4]{0,1:T(4,128)S(1)}, s32[2048]{0:T(1024)S(1)}, s32[256]{0:T(256)S(1)}, bf16[512,8,128]{2,1,0:T(8,128)(2,1)S(1)}, /*index=5*/bf16[2048,8,128]{2,0,1:T(8,128)(2,1)}, ...), branch_computations={%region_7.9_spmd, %region_8.13_spmd} | conditional | flops 2203581184 | bytes 133766192 | solution.py:53
  125.3 1.4 compare_and_fusion.1
  126.9 4.4 %fusion.14 = (f32[256,8]{0,1:T(8,128)S(1)}, f32[8,2048,256]{2,1,0:T(8,128)S(1)}) fusion(pred[256,2048]{0,1:T(8,128)(4,1)S(1)} %compare_and_fusion.1, bf16[2048,8,128]{2,0,1:T(8,128)(2,1)} %get-tuple-element.46, bf16[512,8,128]{2,0,1:T(8,128)(2,1)S(1)} %copy.54), kind=kOutput, calls=%fused_computation.19 | convolution fusion | flops 1086322688 | bytes 22028288 | tf_op jit(solution)/shard_map/cond/branch_1_fun/qhd,khd->qhk/dot_general | solution.py:32
  131.4 5.7 %copy-done = f32[8,2048,256]{2,1,0:T(8,128)} copy-done((f32[8,2048,256]{2,1,0:T(8,128)}, f32[8,2048,256]{2,1,0:T(8,128)S(1)}, u32[]{:S(2)}) %copy-start) | copy-done | bytes 16777240 | tf_op jit(solution)/shard_map/cond
  137.1 4.0 %fusion.16 = f32[256,8]{0,1:T(8,128)S(1)} fusion(f32[8,2048,256]{2,1,0:T(8,128)S(1)} %get-tuple-element.146, f32[256,8]{0,1:T(8,128)S(1)} %broadcast_maximum_fusion.1, pred[256,2048]{0,1:T(8,128)(4,1)S(1)} %compare_and_fusion.1), kind=kLoop, calls=%fused_computation.21 | loop fusion | flops 20969472 | bytes 17317888 | tf_op jit(solution)/shard_map/cond/branch_1_fun/reduce_sum | solution.py:40
  141.1 10.3 %fusion.20 = f32[256,8,128]{2,0,1:T(8,128)S(1)} fusion(bf16[2048,8,128]{2,0,1:T(8,128)(2,1)} %get-tuple-element.48, f32[8,2048,256]{2,1,0:T(8,128)} %copy-done, f32[256,8]{0,1:T(8,128)S(1)} %broadcast_maximum_fusion.1, pred[256,2048]{0,1:T(8,128)(4,1)S(1)} %compare_and_fusion.1), kind=kOutput, calls=%fused_computation.25 | convolution fusion | flops 1094713344 | bytes 22552576 | tf_op jit(solution)/shard_map/cond/branch_1_fun/qhk,khd->qhd/dot_general | solution.py:41
  152.1 26.9 %conditional.2 = (f32[256,8]{0,1:T(8,128)S(1)}, f32[256,8,128]{2,1,0:T(8,128)S(1)}) conditional(s32[]{:T(128)} %bitcast.4, () %tuple.25, (s32[2048]{0:T(1024)S(1)}, s32[256,4]{0,1:T(4,128)S(1)}, s32[2048]{0:T(1024)S(1)}, s32[256]{0:T(256)S(1)}, bf16[512,8,128]{2,1,0:T(8,128)(2,1)S(1)}, /*index=5*/bf16[2048,8,128]{2,0,1:T(8,128)(2,1)}, ...), branch_computations={%region_2.4_spmd, %region_3.0_spmd} | conditional | flops 2203581184 | bytes 133766192 | solution.py:53
  152.4 1.4 compare_and_fusion
  154.0 4.4 %fusion = (f32[256,8]{0,1:T(8,128)S(1)}, f32[8,2048,256]{2,1,0:T(8,128)S(1)}) fusion(pred[256,2048]{0,1:T(8,128)(4,1)S(1)} %compare_and_fusion, bf16[2048,8,128]{2,0,1:T(8,128)(2,1)} %get-tuple-element.39, bf16[512,8,128]{2,0,1:T(8,128)(2,1)S(1)} %copy.51), kind=kOutput, calls=%fused_computation.4 | convolution fusion | flops 1086322688 | bytes 22028288 | tf_op jit(solution)/shard_map/cond/branch_1_fun/qhd,khd->qhk/dot_general | solution.py:32
  158.4 5.7 %copy-done.1 = f32[8,2048,256]{2,1,0:T(8,128)} copy-done((f32[8,2048,256]{2,1,0:T(8,128)}, f32[8,2048,256]{2,1,0:T(8,128)S(1)}, u32[]{:S(2)}) %copy-start.1) | copy-done | bytes 16777240 | tf_op jit(solution)/shard_map/cond
  164.1 4.0 %fusion.2 = f32[256,8]{0,1:T(8,128)S(1)} fusion(f32[8,2048,256]{2,1,0:T(8,128)S(1)} %get-tuple-element.144, f32[256,8]{0,1:T(8,128)S(1)} %broadcast_maximum_fusion, pred[256,2048]{0,1:T(8,128)(4,1)S(1)} %compare_and_fusion), kind=kLoop, calls=%fused_computation.6 | loop fusion | flops 20969472 | bytes 17317888 | tf_op jit(solution)/shard_map/cond/branch_1_fun/reduce_sum | solution.py:40
  168.1 10.3 %fusion.6 = f32[256,8,128]{2,0,1:T(8,128)S(1)} fusion(bf16[2048,8,128]{2,0,1:T(8,128)(2,1)} %get-tuple-element.41, f32[8,2048,256]{2,1,0:T(8,128)} %copy-done.1, f32[256,8]{0,1:T(8,128)S(1)} %broadcast_maximum_fusion, pred[256,2048]{0,1:T(8,128)(4,1)S(1)} %compare_and_fusion), kind=kOutput, calls=%fused_computation.10 | convolution fusion | flops 1094713344 | bytes 22552576 | tf_op jit(solution)/shard_map/cond/branch_1_fun/qhk,khd->qhd/dot_general | solution.py:41
  (37 shorter events, 10.5 us)
Async XLA Ops:
  7.2 58.0 %all-gather.5.cloned.1.call-start = ((), (), s32[]{:S(2)}) async-start(), calls=%async_computation.2 | async-start | bytes 2621440 | tf_op jit(solution)/shard_map/all_gather | solution.py:88
  9.1 104.0 %all-gather.3.cloned.1.call-start = ((), (), s32[]{:S(2)}) async-start(), calls=%async_computation.1 | async-start | bytes 2621440 | tf_op jit(solution)/shard_map/all_gather | solution.py:87
  16.7 28.8 %all-to-all-start = ((bf16[4,2,32768]{2,1,0:T(2,128)(2,1)}), bf16[4,2,32768]{2,1,0:T(2,128)(2,1)S(1)}, u32[]{:S(2)}, u32[]{:S(2)}) async-start(bf16[4,2,32768]{2,1,0:T(2,128)(2,1)} %reshape.190), calls=%async_computation | async-start | bytes 1048576 | tf_op jit(solution)/shard_map/all_to_all | solution.py:105
  50.7 74.6 %copy-start.2 = (bf16[512,8,128]{2,1,0:T(8,128)(2,1)S(1)}, bf16[512,8,128]{2,1,0:T(8,128)(2,1)}, u32[]{:S(2)}) copy-start(bf16[512,8,128]{2,1,0:T(8,128)(2,1)} %param.11) | copy-start | bytes 3145732
  131.3 5.7 %copy-start = (f32[8,2048,256]{2,1,0:T(8,128)}, f32[8,2048,256]{2,1,0:T(8,128)S(1)}, u32[]{:S(2)}) copy-start(f32[8,2048,256]{2,1,0:T(8,128)S(1)} %get-tuple-element.146) | copy-start | bytes 50331652 | tf_op jit(solution)/shard_map/cond
  158.4 5.7 %copy-start.1 = (f32[8,2048,256]{2,1,0:T(8,128)}, f32[8,2048,256]{2,1,0:T(8,128)S(1)}, u32[]{:S(2)}) copy-start(f32[8,2048,256]{2,1,0:T(8,128)S(1)} %get-tuple-element.144) | copy-start | bytes 50331652 | tf_op jit(solution)/shard_map/cond
Sparse Core Ops, SparseCore 0:
  10.1 55.0 all-gather.4
  66.8 46.3 all-gather.2
where the time goes:
time: 191 us; the launch traced here: 188 us
  waiting for transfers between devices  78.7 us (41%)
  local copies, waits for them, and re-layouts  31.2 us (16%)
  matrix products  30.5 us (16%)
  other arithmetic  27 us (14%)
  between operations  15.3 us (8%)
  starting transfers between devices  4.72 us (2%)
    all_gather x1, waiting for transfers between devices, body(): lax.all_gather(keys, 'ctx', axis=0, tiled=True)  43.4 us
    all_to_all x1, waiting for transfers between devices, body(): lax.all_to_all(outgoing, 'ctx', split_axis=0, concat_axis=0, tiled=True)  20.9 us
    dot_general x2, matrix products, compute(): jnp.einsum('qhk,khd->qhd', weight.astype(jnp.bfloat16), value_piece, pref...  20.6 us
    all_gather x1, waiting for transfers between devices, body(): lax.all_gather(values, 'ctx', axis=0, tiled=True)  14.5 us
    cond x4, local copies, waits for them, and re-layouts  11.4 us
    dot_general x2, matrix products, compute(): jnp.einsum('qhd,khd->qhk', query_half, key_piece, preferred_element_type=...  8.84 us
    reduce_sum x2, other arithmetic, compute(): denom = jnp.sum(weight, axis=2)  8.01 us
    select_n x1, other arithmetic, absorb(): value_piece = jnp.take(pieces[1], kv_index, axis=1)  7.49 us
  transfers between devices with their start and end apart: 3, of which 3 were waited for; matrix products, arithmetic and copies ran while one was open for 10% of the time, Pallas kernels for 0%

commit v1 on v0

v1 whole, which is shorter than its diff:
```python
import functools
import math

import jax
import jax.numpy as jnp
from jax import lax
from jax.experimental import pallas as pl
from jax.experimental.pallas import tpu as pltpu
from jax.sharding import PartitionSpec as P

PAGE = 128
MESH = pl.DeviceIdType.MESH
NEG = -1e30


def wide(x, lanes):
    return jnp.concatenate([x] * (lanes // 128), axis=1) if lanes > 128 else x


def kernel(
    n, window, heads, group, lengths, ranks, q_ref, kv_ref, out_ref, dec_ref,
    buf, mask_tx, mask_rx, stage, start_ref, acc, peak, total,
    z_send, z_recv, c_send, c_recv, m_send, m_recv, p_send, p_recv,
):
    me = lax.axis_index("ctx")
    core = lax.axis_index("rep")
    tok, kvw = kv_ref.shape[1:]
    half = tok // 2
    pages = tok // PAGE
    factor = 128 ** -0.5 * math.log2(math.e)

    barrier = pltpu.get_barrier_semaphore()
    for step in range(1, n):
        pl.semaphore_signal(
            barrier, inc=1, device_id={"ctx": lax.rem(me + step, n)}, device_id_type=MESH
        )
    pl.semaphore_signal(barrier, inc=1, device_id={"rep": 1 - core}, device_id_type=MESH)
    pl.semaphore_wait(barrier, n)

    def rows(part):
        return pl.ds(part * half, half)

    def block_copy(d, part):
        return pltpu.make_async_remote_copy(
            src_ref=kv_ref.at[core, rows(part)],
            dst_ref=buf.at[core, d - 1, rows(part)],
            send_sem=z_send.at[d - 1, part],
            recv_sem=z_recv.at[d - 1, part],
            device_id={"ctx": lax.rem(me + d, n)},
            device_id_type=MESH,
        )

    def core_copy(d, part, which):
        return pltpu.make_async_remote_copy(
            src_ref=buf.at[which, d - 1, rows(part)],
            dst_ref=buf.at[which, d - 1, rows(part)],
            send_sem=c_send.at[d - 1, part],
            recv_sem=c_recv.at[d - 1, part],
            device_id={"rep": 1 - core},
            device_id_type=MESH,
        )

    def mask_copy(d):
        return pltpu.make_async_remote_copy(
            src_ref=mask_tx.at[d - 1],
            dst_ref=mask_rx.at[d - 1],
            send_sem=m_send.at[d - 1],
            recv_sem=m_recv.at[d - 1],
            device_id={"ctx": lax.rem(me + d, n)},
            device_id_type=MESH,
        )

    def page_copy(there, slot):
        return pltpu.make_async_remote_copy(
            src_ref=stage.at[there],
            dst_ref=dec_ref.at[slot],
            send_sem=p_send.at[there],
            recv_sem=p_recv.at[slot],
            device_id={"ctx": there},
            device_id_type=MESH,
        )

    def page_for(rank):
        page = jnp.zeros((PAGE, kvw), jnp.bfloat16)
        for g in range(pages):
            flag = jnp.where(ranks[g] == rank, jnp.float32(1), jnp.float32(0))
            flag = jnp.full((PAGE, kvw), flag, jnp.float32).astype(jnp.bfloat16)
            page = page + flag * kv_ref[core, pl.ds(g * PAGE, PAGE), :]
        return page

    def start_blocks(d):
        @pl.when(me + d < n)
        def _():
            for part in (1, 0):
                block_copy(d, part).start()

    start_blocks(1)
    mask_tx[...] = jnp.zeros_like(mask_tx)

    for there in range(n):
        @pl.when((there < me) | (there > me + window))
        def _(there=there):
            stage[there] = page_for(there)
            page_copy(there, me).start()

    for d in range(1, window + 1):
        @pl.when(me + d < n)
        def _(d=d):
            for g in range(pages):
                chosen = jnp.where(ranks[g] == me + d, jnp.float32(1), jnp.float32(0))
                mask_tx[d - 1, g : g + 1, :] = jnp.full((1, 128), chosen, jnp.float32)
            mask_copy(d).start()

    dec_ref[me] = page_for(me)

    pos = me * tok + lax.broadcasted_iota(jnp.int32, (tok, 128), 0)
    first = jnp.zeros((tok, 128), jnp.int32)
    end = jnp.int32(0)
    for r in range(lengths.shape[0]):
        end = end + lengths[r]
        first = jnp.where(pos >= end, end, first)
    start_ref[...] = first

    def attend(keys_at, values_at, base, k0, kn, q0, qn, own):
        def one(h, carry):
            lane = pl.ds(pl.multiple_of(((core * heads + h) // group) * 128, 128), 128)
            mine = pl.ds(pl.multiple_of(h * 128, 128), 128)
            k = keys_at[pl.ds(k0, kn), lane]
            v = values_at[pl.ds(k0, kn), lane]
            score = lax.dot_general(
                q_ref[pl.ds(q0, qn), mine], k, (((1,), (1,)), ((), ())),
                preferred_element_type=jnp.float32,
            )
            key_pos = base + k0 + lax.broadcasted_iota(jnp.int32, (qn, kn), 1)
            allowed = key_pos >= wide(start_ref[pl.ds(q0, qn), :], kn)
            if own:
                query_pos = base + q0 + lax.broadcasted_iota(jnp.int32, (qn, kn), 0)
                allowed = allowed & (key_pos <= query_pos)
            score = jnp.where(allowed, score, NEG)
            top = jnp.broadcast_to(jnp.max(score, axis=1, keepdims=True), (qn, 128))
            span = pl.ds(q0, qn)
            if not own:
                old = peak[h, span, :]
                top = jnp.maximum(old, top)
            weight = jnp.exp2((score - wide(top, kn)) * factor)
            part = weight[:, :128]
            for c in range(128, kn, 128):
                part = part + weight[:, c : c + 128]
            mixed = jnp.dot(weight.astype(jnp.bfloat16), v, preferred_element_type=jnp.float32)
            if not own:
                keep = jnp.exp2((old - top) * factor)
                part = part + keep * total[h, span, :]
                mixed = mixed + keep * acc[h, span, :]
            peak[h, span, :] = top
            total[h, span, :] = part
            acc[h, span, :] = mixed
            return carry

        lax.fori_loop(0, heads, one, 0, unroll=2)

    mine_k, mine_v = kv_ref.at[0], kv_ref.at[1]
    attend(mine_k, mine_v, me * tok, 0, half, 0, half, True)
    attend(mine_k, mine_v, me * tok, 0, tok, half, half, True)

    for d in range(1, window + 1):
        @pl.when(me + d < n)
        def _(d=d):
            for part in (1, 0):
                block_copy(d, part).wait_send()

        if d < window:
            start_blocks(d + 1)

        @pl.when(me >= d)
        def _(d=d):
            base = (me - d) * tok
            for part in (1, 0):
                block_copy(d, part).wait_recv()
                core_copy(d, part, core).start()
                core_copy(d, part, 1 - core).wait_recv()
                shorter = d == window and part == 0 and 2 * window == n
                attend(
                    buf.at[0, d - 1], buf.at[1, d - 1], base, part * half, half,
                    0, half if shorter else tok, False,
                )
            mask_copy(d).wait_recv()
            chosen = jnp.zeros((PAGE, kvw), jnp.bfloat16)
            for g in range(pages):
                flag = jnp.broadcast_to(mask_rx[d - 1, g : g + 1, :], (PAGE, 128))
                chosen = chosen + wide(flag.astype(jnp.bfloat16), kvw) * buf[
                    core, d - 1, pl.ds(g * PAGE, PAGE), :
                ]
            dec_ref[me - d] = chosen
            for part in (1, 0):
                core_copy(d, part, core).wait_send()

    def finish(h, carry):
        mine = pl.ds(pl.multiple_of(h * 128, 128), 128)
        whole = jnp.sum(total[h], axis=1, keepdims=True)
        out_ref[:, mine] = (acc[h] / whole).astype(jnp.bfloat16)
        return carry

    lax.fori_loop(0, heads, finish, 0)

    for d in range(1, window + 1):
        @pl.when(me + d < n)
        def _(d=d):
            mask_copy(d).wait_send()

    for other in range(n):
        @pl.when((other < me) | (other > me + window))
        def _(other=other):
            page_copy(other, me).wait_send()

        @pl.when((other > me) | (other < me - window))
        def _(other=other):
            page_copy(other, other).wait_recv()


def body(queries, keys, values, lengths, page_ranks):
    tok, heads, dim = queries.shape
    kv_heads = keys.shape[1]
    n = lax.axis_size("ctx")
    rep = lax.axis_size("rep")
    window = n // 2
    group = heads * rep // kv_heads
    kvw = kv_heads * dim
    kv = jnp.stack([keys.reshape(tok, kvw), values.reshape(tok, kvw)])
    vmem = pl.BlockSpec(memory_space=pltpu.VMEM)
    smem = pl.BlockSpec(memory_space=pltpu.SMEM)
    flag_rows = -(-(tok // PAGE) // 8) * 8
    dma = pltpu.SemaphoreType.DMA
    context, cache = pl.pallas_call(
        functools.partial(kernel, n, window, heads, group),
        out_shape=(
            jax.ShapeDtypeStruct((tok, heads * dim), jnp.bfloat16),
            jax.ShapeDtypeStruct((n, PAGE, kvw), jnp.bfloat16),
        ),
        in_specs=[smem, smem, vmem, vmem],
        out_specs=(vmem, vmem),
        scratch_shapes=[
            pltpu.VMEM((2, window, tok, kvw), jnp.bfloat16),
            pltpu.VMEM((window, flag_rows, 128), jnp.float32),
            pltpu.VMEM((window, flag_rows, 128), jnp.float32),
            pltpu.VMEM((n, PAGE, kvw), jnp.bfloat16),
            pltpu.VMEM((tok, 128), jnp.int32),
            pltpu.VMEM((heads, tok, 128), jnp.float32),
            pltpu.VMEM((heads, tok, 128), jnp.float32),
            pltpu.VMEM((heads, tok, 128), jnp.float32),
            dma((window, 2)),
            dma((window, 2)),
            dma((window, 2)),
            dma((window, 2)),
            dma((window,)),
            dma((window,)),
            dma((n,)),
            dma((n,)),
        ],
        compiler_params=pltpu.CompilerParams(
            collective_id=0, has_side_effects=True, vmem_limit_bytes=48 * 1024 * 1024
        ),
        cost_estimate=pl.CostEstimate(
            flops=4 * heads * tok * tok * 2 * dim, bytes_accessed=8 * tok * kvw,
            transcendentals=heads * tok * tok * 2,
        ),
    )(lengths, page_ranks, queries.reshape(tok, heads * dim), kv)
    return (
        context.reshape(tok, heads, dim),
        cache.reshape(1, n, PAGE, 1, kv_heads, dim),
    )


def solution(mesh):
    in_specs = (
        P(("groups", "ctx"), ("tp", "rep"), None),
        P(("groups", "ctx"), "tp", None),
        P(("groups", "ctx"), "tp", None),
        P("groups"),
        P(("groups", "ctx")),
    )
    out_specs = (
        P(("groups", "ctx"), ("tp", "rep"), None),
        P(("groups", "ctx"), None, None, "rep", "tp", None),
    )
    return jax.shard_map(body, mesh=mesh, in_specs=in_specs, out_specs=out_specs, check_vma=False)
```

time: 191 us -> 53.4 us (0.28)
  the two profiles are of different devices: /device:TPU:17 before, /device:TPU:27 now
where the time goes in v1:
time: 53.4 us; the launch traced here: 53.2 us
  Pallas kernels  46.7 us (87%)
  local copies, waits for them, and re-layouts  5.71 us (11%)
  between operations  0.71 us (1%)
    pallas_call x1, Pallas kernels, body(): pl.pallas_call(functools.partial(kernel, n, window, heads, group), out_sh...  46.7 us
    unnamed x10, local copies, waits for them, and re-layouts  3.29 us
    another operation x2, local copies, waits for them, and re-layouts, body(): kv = jnp.stack([keys.reshape(tok, kvw), values.reshape(tok, kvw)])  1.5 us

profile of v1, /device:TPU:27, one launch (start us, length us, event | category | flops | bytes accessed | tf_op | source)
XLA Modules:
  0.0 53.2 jit_solution(3883567364861202917)
XLA Ops:
  0.6 0.0 copy-start.3
  0.6 1.3 %stack_reshape.6 = bf16[1,512,512]{2,1,0:T(8,128)(2,1)S(1)} reshape(bf16[512,4,128]{2,1,0:T(4,128)(2,1)} %param.6) | data formatting | bytes 1048576 | tf_op jit(solution)/shard_map/stack;reshape | solution.py:228
  1.9 0.0 copy-done.3
  1.9 0.2 stack_reshape.7
  2.2 0.0 copy-start.2
  2.2 0.1 pad_maximum_fusion.kv_ref
  2.3 1.1 %copy-done.2 = bf16[512,8,128]{2,1,0:T(8,128)(2,1)S(1)} copy-done((bf16[512,8,128]{2,1,0:T(8,128)(2,1)S(1)}, bf16[512,8,128]{2,1,0:T(8,128)(2,1)}, u32[]{:S(2)}) %copy-start.2) | copy-done | bytes 1048600
  3.4 0.3 copy.11
  3.7 0.0 copy-start
  3.7 0.0 copy-start.1
  3.7 0.6 %copy-done = s32[4]{0:T(128)S(1)} copy-done((s32[4]{0:T(128)S(1)}, s32[4]{0:T(128)}, u32[]{:S(2)}) %copy-start) | copy-done | bytes 40
  4.3 0.0 copy-done.1
  4.3 46.7 %shard_map.68 = (bf16[512,1024]{1,0:T(8,128)(2,1)S(1)}, bf16[4,128,512]{2,1,0:T(8,128)(2,1)S(1)}) custom-call(s32[4]{0:T(128)S(1)} %copy-done, s32[4]{0:T(128)S(1)} %copy-done.1, bf16[512,1024]{1,0:T(8,128)(2,1)S(1)} %bitcast.8, bf16[2,512,512]{2,1,0:T(8,128)(2,1)S(1)} %pad_maximum_fusion.kv_ref), custom_call_target="tpu_custom_call" | custom-call | flops 2147483648 | bytes 2097152 | tf_op jit(solution)/shard_map/pallas_call | solution.py:233
  51.0 1.2 %copy.9 = bf16[64,8,8,128]{3,2,1,0:T(8,128)(2,1)} copy(bf16[64,8,8,128]{3,1,2,0:T(8,128)(2,1)S(1)} %bitcast.7) | data formatting | bytes 2097152
  52.3 0.9 %reshape.15 = bf16[1,4,128,1,4,128]{5,4,2,1,3,0:T(4,128)(2,1)} reshape(bf16[4,128,512]{2,1,0:T(8,128)(2,1)S(1)} %get-tuple-element.5) | data formatting | bytes 1048576 | tf_op jit(solution)/shard_map/reshape | solution.py:269
Async XLA Ops:
  0.6 1.3 %copy-start.3 = (bf16[512,4,128]{2,1,0:T(4,128)(2,1)S(1)}, bf16[512,4,128]{2,1,0:T(4,128)(2,1)}, u32[]{:S(2)}) copy-start(bf16[512,4,128]{2,1,0:T(4,128)(2,1)} %param.7) | copy-start | bytes 1572868
  2.2 1.2 %copy-start.2 = (bf16[512,8,128]{2,1,0:T(8,128)(2,1)S(1)}, bf16[512,8,128]{2,1,0:T(8,128)(2,1)}, u32[]{:S(2)}) copy-start(bf16[512,8,128]{2,1,0:T(8,128)(2,1)} %param.5) | copy-start | bytes 3145732
  3.7 0.7 %copy-start = (s32[4]{0:T(128)S(1)}, s32[4]{0:T(128)}, u32[]{:S(2)}) copy-start(s32[4]{0:T(128)} %lengths.1) | copy-start | bytes 52
  3.7 0.7 %copy-start.1 = (s32[4]{0:T(128)S(1)}, s32[4]{0:T(128)}, u32[]{:S(2)}) copy-start(s32[4]{0:T(128)} %ranks.1) | copy-start | bytes 52

commit v2 on v1

--- a/solution.py
+++ b/solution.py
@@ -41,12 +41,13 @@
         return pl.ds(part * half, half)
 
     def block_copy(d, part):
-        return pltpu.make_async_remote_copy(
-            src_ref=kv_ref.at[core, rows(part)],
+        own = kv_ref.at[core, rows(part)]
+        return pltpu.make_async_remote_copy(
+            src_ref=own if d == 1 else buf.at[core, d - 2, rows(part)],
             dst_ref=buf.at[core, d - 1, rows(part)],
             send_sem=z_send.at[d - 1, part],
             recv_sem=z_recv.at[d - 1, part],
-            device_id={"ctx": lax.rem(me + d, n)},
+            device_id={"ctx": lax.rem(me + 1, n)},
             device_id_type=MESH,
         )
 
@@ -88,13 +89,11 @@
             page = page + flag * kv_ref[core, pl.ds(g * PAGE, PAGE), :]
         return page
 
-    def start_blocks(d):
-        @pl.when(me + d < n)
-        def _():
-            for part in (1, 0):
-                block_copy(d, part).start()
-
-    start_blocks(1)
+    @pl.when(me + 1 < n)
+    def _():
+        for part in (1, 0):
+            block_copy(1, part).start()
+
     mask_tx[...] = jnp.zeros_like(mask_tx)
 
     for there in range(n):
@@ -156,27 +155,23 @@
             acc[h, span, :] = mixed
             return carry
 
-        lax.fori_loop(0, heads, one, 0, unroll=2)
+        lax.fori_loop(0, heads, one, 0, unroll=4)
 
     mine_k, mine_v = kv_ref.at[0], kv_ref.at[1]
     attend(mine_k, mine_v, me * tok, 0, half, 0, half, True)
     attend(mine_k, mine_v, me * tok, 0, tok, half, half, True)
 
     for d in range(1, window + 1):
-        @pl.when(me + d < n)
-        def _(d=d):
-            for part in (1, 0):
-                block_copy(d, part).wait_send()
-
-        if d < window:
-            start_blocks(d + 1)
-
         @pl.when(me >= d)
         def _(d=d):
             base = (me - d) * tok
             for part in (1, 0):
                 block_copy(d, part).wait_recv()
                 core_copy(d, part, core).start()
+                if d < window:
+                    @pl.when(me + 1 < n)
+                    def _(part=part):
+                        block_copy(d + 1, part).start()
                 core_copy(d, part, 1 - core).wait_recv()
                 shorter = d == window and part == 0 and 2 * window == n
                 attend(
@@ -206,6 +201,11 @@
         @pl.when(me + d < n)
         def _(d=d):
             mask_copy(d).wait_send()
+
+        @pl.when((me + 1 < n) & (me >= d - 1))
+        def _(d=d):
+            for part in (1, 0):
+                block_copy(d, part).wait_send()
 
     for other in range(n):
         @pl.when((other < me) | (other > me + window))

time: 53.4 us -> 41.2 us (0.77)
  the two profiles are of different devices: /device:TPU:27 before, /device:TPU:17 now
where the time goes in v2:
time: 41.2 us; the launch traced here: 41 us
  Pallas kernels  34.5 us (84%)
  local copies, waits for them, and re-layouts  5.71 us (14%)
  between operations  0.71 us (2%)
    pallas_call x1, Pallas kernels, body(): pl.pallas_call(functools.partial(kernel, n, window, heads, group), out_sh...  34.5 us
    unnamed x10, local copies, waits for them, and re-layouts  3.29 us
    another operation x2, local copies, waits for them, and re-layouts, body(): kv = jnp.stack([keys.reshape(tok, kvw), values.reshape(tok, kvw)])  1.5 us
    reshape x1, local copies, waits for them, and re-layouts, body(): cache.reshape(1, n, PAGE, 1, kv_heads, dim)  0.92 us

profile of v2, /device:TPU:17, one launch (start us, length us, event | category | flops | bytes accessed | tf_op | source)
XLA Modules:
  0.0 41.0 jit_solution(1437576335983546086)
XLA Ops:
  0.6 0.0 copy-start.3
  0.6 1.3 %stack_reshape.6 = bf16[1,512,512]{2,1,0:T(8,128)(2,1)S(1)} reshape(bf16[512,4,128]{2,1,0:T(4,128)(2,1)} %param.6) | data formatting | bytes 1048576 | tf_op jit(solution)/shard_map/stack;reshape | solution.py:228
  1.9 0.0 copy-done.3
  1.9 0.2 stack_reshape.7
  2.2 0.0 copy-start.2
  2.2 0.1 pad_maximum_fusion.kv_ref
  2.3 1.1 %copy-done.2 = bf16[512,8,128]{2,1,0:T(8,128)(2,1)S(1)} copy-done((bf16[512,8,128]{2,1,0:T(8,128)(2,1)S(1)}, bf16[512,8,128]{2,1,0:T(8,128)(2,1)}, u32[]{:S(2)}) %copy-start.2) | copy-done | bytes 1048600
  3.4 0.3 copy.11
  3.7 0.0 copy-start
  3.7 0.0 copy-start.1
  3.7 0.6 %copy-done = s32[4]{0:T(128)S(1)} copy-done((s32[4]{0:T(128)S(1)}, s32[4]{0:T(128)}, u32[]{:S(2)}) %copy-start) | copy-done | bytes 40
  4.3 0.0 copy-done.1
  4.3 34.5 %shard_map.68 = (bf16[512,1024]{1,0:T(8,128)(2,1)S(1)}, bf16[4,128,512]{2,1,0:T(8,128)(2,1)S(1)}) custom-call(s32[4]{0:T(128)S(1)} %copy-done, s32[4]{0:T(128)S(1)} %copy-done.1, bf16[512,1024]{1,0:T(8,128)(2,1)S(1)} %bitcast.8, bf16[2,512,512]{2,1,0:T(8,128)(2,1)S(1)} %pad_maximum_fusion.kv_ref), custom_call_target="tpu_custom_call" | custom-call | flops 2147483648 | bytes 2097152 | tf_op jit(solution)/shard_map/pallas_call | solution.py:233
  38.9 1.2 %copy.9 = bf16[64,8,8,128]{3,2,1,0:T(8,128)(2,1)} copy(bf16[64,8,8,128]{3,1,2,0:T(8,128)(2,1)S(1)} %bitcast.7) | data formatting | bytes 2097152
  40.1 0.9 %reshape.15 = bf16[1,4,128,1,4,128]{5,4,2,1,3,0:T(4,128)(2,1)} reshape(bf16[4,128,512]{2,1,0:T(8,128)(2,1)S(1)} %get-tuple-element.5) | data formatting | bytes 1048576 | tf_op jit(solution)/shard_map/reshape | solution.py:269
Async XLA Ops:
  0.6 1.3 %copy-start.3 = (bf16[512,4,128]{2,1,0:T(4,128)(2,1)S(1)}, bf16[512,4,128]{2,1,0:T(4,128)(2,1)}, u32[]{:S(2)}) copy-start(bf16[512,4,128]{2,1,0:T(4,128)(2,1)} %param.7) | copy-start | bytes 1572868
  2.2 1.2 %copy-start.2 = (bf16[512,8,128]{2,1,0:T(8,128)(2,1)S(1)}, bf16[512,8,128]{2,1,0:T(8,128)(2,1)}, u32[]{:S(2)}) copy-start(bf16[512,8,128]{2,1,0:T(8,128)(2,1)} %param.5) | copy-start | bytes 3145732
  3.7 0.7 %copy-start = (s32[4]{0:T(128)S(1)}, s32[4]{0:T(128)}, u32[]{:S(2)}) copy-start(s32[4]{0:T(128)} %lengths.1) | copy-start | bytes 52
  3.7 0.7 %copy-start.1 = (s32[4]{0:T(128)S(1)}, s32[4]{0:T(128)}, u32[]{:S(2)}) copy-start(s32[4]{0:T(128)} %ranks.1) | copy-start | bytes 52

commit v3 on v2

--- a/solution.py
+++ b/solution.py
@@ -18,8 +18,8 @@
 
 
 def kernel(
-    n, window, heads, group, lengths, ranks, q_ref, kv_ref, out_ref, dec_ref,
-    buf, mask_tx, mask_rx, stage, start_ref, acc, peak, total,
+    n, window, heads, group, lengths, ranks, queries_ref, kv_ref, out_ref, dec_ref,
+    q_raw, q_ref, q_sem, buf, mask_tx, mask_rx, stage, start_ref, acc, peak, total,
     z_send, z_recv, c_send, c_recv, m_send, m_recv, p_send, p_recv,
 ):
     me = lax.axis_index("ctx")
@@ -29,6 +29,8 @@
     pages = tok // PAGE
     factor = 128 ** -0.5 * math.log2(math.e)
 
+    fetch = pltpu.make_async_copy(queries_ref, q_raw, q_sem)
+    fetch.start()
     barrier = pltpu.get_barrier_semaphore()
     for step in range(1, n):
         pl.semaphore_signal(
@@ -157,6 +159,10 @@
 
         lax.fori_loop(0, heads, one, 0, unroll=4)
 
+    fetch.wait()
+    for h in range(heads):
+        q_ref[:, h * 128 : (h + 1) * 128] = q_raw[:, h, :]
+
     mine_k, mine_v = kv_ref.at[0], kv_ref.at[1]
     attend(mine_k, mine_v, me * tok, 0, half, 0, half, True)
     attend(mine_k, mine_v, me * tok, 0, tok, half, half, True)
@@ -195,7 +201,7 @@
         out_ref[:, mine] = (acc[h] / whole).astype(jnp.bfloat16)
         return carry
 
-    lax.fori_loop(0, heads, finish, 0)
+    lax.fori_loop(0, heads, finish, 0, unroll=2)
 
     for d in range(1, window + 1):
         @pl.when(me + d < n)
@@ -236,9 +242,12 @@
             jax.ShapeDtypeStruct((tok, heads * dim), jnp.bfloat16),
             jax.ShapeDtypeStruct((n, PAGE, kvw), jnp.bfloat16),
         ),
-        in_specs=[smem, smem, vmem, vmem],
+        in_specs=[smem, smem, pl.BlockSpec(memory_space=pl.ANY), vmem],
         out_specs=(vmem, vmem),
         scratch_shapes=[
+            pltpu.VMEM((tok, heads, dim), jnp.bfloat16),
+            pltpu.VMEM((tok, heads * dim), jnp.bfloat16),
+            dma,
             pltpu.VMEM((2, window, tok, kvw), jnp.bfloat16),
             pltpu.VMEM((window, flag_rows, 128), jnp.float32),
             pltpu.VMEM((window, flag_rows, 128), jnp.float32),
@@ -263,7 +272,7 @@
             flops=4 * heads * tok * tok * 2 * dim, bytes_accessed=8 * tok * kvw,
             transcendentals=heads * tok * tok * 2,
         ),
-    )(lengths, page_ranks, queries.reshape(tok, heads * dim), kv)
+    )(lengths, page_ranks, queries, kv)
     return (
         context.reshape(tok, heads, dim),
         cache.reshape(1, n, PAGE, 1, kv_heads, dim),

time: 41.2 us -> 40 us (0.971)
  local copies, waits for them, and re-layouts: 5.71 us -> 4.77 us
    unnamed x10 -> x9, local copies, waits for them, and re-layouts: 3.29 us -> 2.35 us
where the time goes in v3:
time: 40 us; the launch traced here: 39.8 us
  Pallas kernels  34.3 us (86%)
  local copies, waits for them, and re-layouts  4.77 us (12%)
  between operations  0.7 us (2%)
    pallas_call x1, Pallas kernels, body(): pl.pallas_call(functools.partial(kernel, n, window, heads, group), out_sh...  34.3 us
    unnamed x9, local copies, waits for them, and re-layouts  2.35 us
    another operation x2, local copies, waits for them, and re-layouts, body(): kv = jnp.stack([keys.reshape(tok, kvw), values.reshape(tok, kvw)])  1.5 us
    reshape x1, local copies, waits for them, and re-layouts, body(): cache.reshape(1, n, PAGE, 1, kv_heads, dim)  0.92 us

profile of v3, /device:TPU:17, one launch (start us, length us, event | category | flops | bytes accessed | tf_op | source)
XLA Modules:
  0.0 39.8 jit_solution(209798034704824484)
XLA Ops:
  0.6 0.0 copy-start.3
  0.6 1.3 %stack_reshape.6 = bf16[1,512,512]{2,1,0:T(8,128)(2,1)S(1)} reshape(bf16[512,4,128]{2,1,0:T(4,128)(2,1)} %param.6) | data formatting | bytes 1048576 | tf_op jit(solution)/shard_map/stack;reshape | solution.py:234
  1.9 0.0 copy-done.3
  1.9 0.2 stack_reshape.7
  2.2 0.0 copy-start
  2.2 0.0 copy-start.1
  2.2 0.0 copy-start.2
  2.2 0.1 pad_maximum_fusion.kv_ref
  2.3 1.1 %copy-done = bf16[512,8,128]{2,1,0:T(8,128)(2,1)S(1)} copy-done((bf16[512,8,128]{2,1,0:T(8,128)(2,1)S(1)}, bf16[512,8,128]{2,1,0:T(8,128)(2,1)}, u32[]{:S(2)}) %copy-start) | copy-done | bytes 1048600
  3.4 0.0 copy-done.1
  3.4 0.0 copy-done.2
  3.4 34.3 %shard_map.68 = (bf16[512,1024]{1,0:T(8,128)(2,1)S(1)}, bf16[4,128,512]{2,1,0:T(8,128)(2,1)S(1)}) custom-call(s32[4]{0:T(128)S(1)} %copy-done.1, s32[4]{0:T(128)S(1)} %copy-done.2, bf16[512,8,128]{2,1,0:T(8,128)(2,1)S(1)} %copy-done, bf16[2,512,512]{2,1,0:T(8,128)(2,1)S(1)} %pad_maximum_fusion.kv_ref), custom_call_target="tpu_custom_call" | custom-call | flops 2147483648 | bytes 2097152 | tf_op jit(solution)/shard_map/pallas_call | solution.py:239
  37.7 1.2 %copy.8 = bf16[64,8,8,128]{3,2,1,0:T(8,128)(2,1)} copy(bf16[64,8,8,128]{3,1,2,0:T(8,128)(2,1)S(1)} %bitcast.3) | data formatting | bytes 2097152
  38.9 0.9 %reshape.11 = bf16[1,4,128,1,4,128]{5,4,2,1,3,0:T(4,128)(2,1)} reshape(bf16[4,128,512]{2,1,0:T(8,128)(2,1)S(1)} %get-tuple-element.5) | data formatting | bytes 1048576 | tf_op jit(solution)/shard_map/reshape | solution.py:278
Async XLA Ops:
  0.6 1.3 %copy-start.3 = (bf16[512,4,128]{2,1,0:T(4,128)(2,1)S(1)}, bf16[512,4,128]{2,1,0:T(4,128)(2,1)}, u32[]{:S(2)}) copy-start(bf16[512,4,128]{2,1,0:T(4,128)(2,1)} %param.7) | copy-start | bytes 1572868
  2.2 1.2 %copy-start = (bf16[512,8,128]{2,1,0:T(8,128)(2,1)S(1)}, bf16[512,8,128]{2,1,0:T(8,128)(2,1)}, u32[]{:S(2)}) copy-start(bf16[512,8,128]{2,1,0:T(8,128)(2,1)} %queries_ref.1) | copy-start | bytes 3145732
  2.2 1.2 %copy-start.1 = (s32[4]{0:T(128)S(1)}, s32[4]{0:T(128)}, u32[]{:S(2)}) copy-start(s32[4]{0:T(128)} %lengths.1) | copy-start | bytes 52
  2.2 1.2 %copy-start.2 = (s32[4]{0:T(128)S(1)}, s32[4]{0:T(128)}, u32[]{:S(2)}) copy-start(s32[4]{0:T(128)} %ranks.1) | copy-start | bytes 52
